TPU v7x, 256 devices: a whole 4x4x8 slice. The times are simulated.
256 devices in a mesh: expert: 32 (over x, z_lo, core), tensor: 8 (over y, z_hi).
Axes of the slice: x: 4, y: 4, z: 8 (z_hi: 2, z_lo: 4; z = z_hi * 4 + z_lo), core: 2. Of those that a mesh axis runs over, the one named last changes fastest.
Arguments:
- prior_gate_weight: bfloat16 [32, 7168, 2048], P('expert', None, 'tensor'), may hold values from -6 to 6
- left_factor: bfloat16 [32, 7168, 64], P('expert'), may hold values from -6 to 6
- right_factor: bfloat16 [32, 64, 2048], P('expert', None, 'tensor'), may hold values from -0.75 to 0.75
- refit_expert_index: int32 [32], replicated, may hold values from 0 to 255, as said below
- placement: int32 [64], replicated, may hold values from 0 to 255, as said below
Outputs:
- slot_gate: bfloat16 [64, 7168, 2048], P('expert', None, 'tensor')
Inputs may be any that keep to these rules, and one draw needn't show every extreme that they name: `refit_expert_index`: 32 distinct routed expert ids. `placement`: every id is one of refit_expert_index; a quarter of the refit experts are hosted by 4 slots, a quarter by 2 and half by 1.
All inputs are finite; a program needn't handle non-finite values.
Results may differ from a plain program's by a relative error of at most 0.001.
Values may be sent and summed in bfloat16 or wider, within the bound.
A program may use at most 64 MiB of HBM per device.

v0:
```python
import jax
import jax.numpy as jnp
from jax import lax
from jax.sharding import PartitionSpec as P

update_scale = 0.5


def merge_expert_block(gate_weight, left, right):
    lowrank_update = jnp.einsum("edr,erf->edf", left, right, preferred_element_type=jnp.float32)
    return (gate_weight.astype(jnp.float32) + update_scale * lowrank_update).astype(jnp.bfloat16)


def per_device(prior_gate_weight, left_factor, right_factor, refit_expert_index, placement):
    refit_count = refit_expert_index.shape[0]
    slot_count = placement.shape[0]
    selector = (placement[:, None] == refit_expert_index[None, :]).astype(jnp.bfloat16)
    merged_gate = merge_expert_block(prior_gate_weight, left_factor, right_factor)
    row_block = lax.all_to_all(merged_gate, "expert", split_axis=1, concat_axis=0, tiled=True)
    depth = row_block.shape[1]
    width = row_block.shape[2]
    flattened = row_block.reshape(refit_count, depth * width)
    picked = jnp.dot(selector, flattened, preferred_element_type=jnp.float32).astype(jnp.bfloat16)
    picked = picked.reshape(slot_count, depth, width)
    return lax.all_to_all(picked, "expert", split_axis=0, concat_axis=1, tiled=True)


def solution(mesh):
    return jax.shard_map(
        per_device,
        mesh=mesh,
        in_specs=(
            P("expert", None, "tensor"),
            P("expert", None, None),
            P("expert", None, "tensor"),
            P(),
            P(),
        ),
        out_specs=P("expert", None, "tensor"),
        check_vma=False,
    )
```

profile of v0, /device:TPU:1, one launch (start us, length us, event | category | flops | bytes accessed | tf_op | source)
XLA Modules:
  0.0 440.5 jit_solution(15327426468417176931)
XLA Ops:
  0.0 0.0 copy-start
  0.0 1.2 copy-done
  1.2 3.2 fusion.2
  4.4 43.4 %copy.13 = bf16[1,7168,256]{2,0,1:T(2,128)(2,1)} copy(bf16[1,7168,256]{2,1,0:T(8,128)(2,1)S(1)} %fusion.2) | data formatting | bytes 7340032 | tf_op jit(solution)/shard_map/convert_element_type | solution.py:11
  47.8 0.5 broadcast.4
  48.3 38.3 %reduce.2 = bf16[7168,256]{1,0:T(8,128)(2,1)} reduce(bf16[7168,1,256]{2,1,0:T(2,128)(2,1)} %bitcast.27, bf16[]{:T(256)} %broadcast.4), dimensions={1}, to_apply=%bitcast.23.reduce_sub_computation | reduce | bytes 7340034
  86.6 8.4 %reshape.25 = bf16[32,2,28672]{2,1,0:T(2,128)(2,1)} reshape(bf16[7168,256]{1,0:T(8,128)(2,1)} %reduce.2) | data formatting | bytes 7340032
  95.0 94.3 %all_to_all.27 = bf16[32,2,28672]{2,1,0:T(2,128)(2,1)} all-to-all(bf16[32,2,28672]{2,1,0:T(2,128)(2,1)} %reshape.25), channel_id=1, replica_groups=mesh['expert'=32,'tensor'=8] {'expert'}, dimensions={0} | all-to-all | bytes 7340032 | tf_op jit(solution)/shard_map/all_to_all | solution.py:19
  189.3 19.2 %reshape.26 = bf16[7168,1,256]{2,1,0:T(2,128)(2,1)} reshape(bf16[32,2,28672]{2,1,0:T(2,128)(2,1)} %all_to_all.27) | data formatting | bytes 7340032
  208.5 0.0 copy-start.2
  208.5 0.0 copy-start.3
  208.5 41.4 %bitcast_reduce_fusion = bf16[7168,256]{1,0:T(8,128)(2,1)} fusion(bf16[7168,1,256]{2,1,0:T(2,128)(2,1)} %reshape.26), kind=kLoop, calls=%fused_computation.10 | loop fusion | bytes 7340032 | tf_op jit(solution)/shard_map/all_to_all | solution.py:19
  249.9 5.2 %reshape.22 = bf16[32,57344]{1,0:T(8,128)(2,1)} reshape(bf16[7168,256]{1,0:T(8,128)(2,1)} %bitcast_reduce_fusion) | data formatting | bytes 7340032 | tf_op jit(solution)/shard_map/reshape | solution.py:22
  255.2 0.0 copy-done.2
  255.2 0.0 copy-done.3
  255.2 7.2 %convolution_convert_fusion = bf16[64,57344]{1,0:T(8,128)(2,1)} fusion(bf16[32,57344]{1,0:T(8,128)(2,1)} %reshape.22, s32[32]{0:T(128)S(1)} %copy-done.2, s32[64]{0:T(128)S(1)} %copy-done.3), kind=kOutput, calls=%fused_computation | convolution fusion | flops 238553088 | bytes 11010432 | tf_op jit(solution)/shard_map/dot_general | solution.py:23
  262.4 5.0 %copy.11 = bf16[8,8,224,256]{3,2,1,0:T(8,128)(2,1)S(1)} copy(bf16[8,8,224,256]{3,1,2,0:T(8,128)(2,1)} %bitcast.26) | data formatting | bytes 14680064
  267.4 166.3 %all_to_all.28 = bf16[64,224,256]{2,1,0:T(8,128)(2,1)} all-to-all(bf16[64,224,256]{2,1,0:T(8,128)(2,1)S(1)} %bitcast.24), channel_id=1, replica_groups=mesh['expert'=32,'tensor'=8] {'expert'}, dimensions={0} | all-to-all | bytes 14680064 | tf_op jit(solution)/shard_map/all_to_all | solution.py:25
  433.7 0.0 copy-start.1
  433.7 6.8 %copy.10 = bf16[32,2,224,256]{3,2,0,1:T(8,128)(2,1)} copy(bf16[32,2,224,256]{3,2,1,0:T(8,128)(2,1)} %bitcast.25) | data formatting | bytes 14680064 | tf_op jit(solution)/shard_map/all_to_all | solution.py:25
  440.5 0.0 copy-done.1
Async XLA Ops:
  0.0 1.2 copy-start
  208.5 46.6 %copy-start.2 = (s32[32]{0:T(128)S(1)}, s32[32]{0:T(128)}, u32[]{:S(2)}) copy-start(s32[32]{0:T(128)} %param.8) | copy-start | bytes 388
  208.5 46.6 %copy-start.3 = (s32[64]{0:T(128)S(1)}, s32[64]{0:T(128)}, u32[]{:S(2)}) copy-start(s32[64]{0:T(128)} %param.9) | copy-start | bytes 772
  433.7 6.8 %copy-start.1 = (bf16[1,7168,64]{1,2,0:T(8,128)(2,1)S(1)}, bf16[1,7168,64]{1,2,0:T(8,128)(2,1)}, u32[]{:S(2)}) copy-start(bf16[1,7168,64]{1,2,0:T(8,128)(2,1)} %param.6) | copy-start | bytes 2752516
where the time goes:
time: 442 us; the launch traced here: 440 us
  blocking collectives  261 us (59%)
  local copies, waits for them, and re-layouts  131 us (30%)
  other arithmetic  38.3 us (9%)
  matrix products  10.4 us (2%)
    all_to_all x1, blocking collectives, per_device(): lax.all_to_all(picked, 'expert', split_axis=0, concat_axis=1, tiled=True)  166 us
    all_to_all x1, blocking collectives, per_device(): lax.all_to_all(merged_gate, 'expert', split_axis=1, concat_axis=0, tiled=...  94.3 us
    convert_element_type x1, local copies, waits for them, and re-layouts, merge_expert_block(): (gate_weight.astype(jnp.float32) + update_scale * lowrank_update).astype(...  43.4 us
    all_to_all x1, local copies, waits for them, and re-layouts, per_device(): lax.all_to_all(merged_gate, 'expert', split_axis=1, concat_axis=0, tiled=...  41.4 us
    unnamed x1, other arithmetic  38.3 us
    unnamed x12, local copies, waits for them, and re-layouts  34.3 us

commit v1 on v0

v1 whole, which is shorter than its diff:
```python
import functools

import jax
import jax.numpy as jnp
from jax import lax
from jax.experimental import pallas as pl
from jax.experimental.pallas import tpu as pltpu
from jax.sharding import PartitionSpec as P

SCALE = 0.5
COLUMNS = 4
ROWS = 4
ROW_EXPERTS = 8
ROW_SLOTS = 16
CHUNK = 32
CAPACITIES = (16,)
ZERO = 32
RING = 4
SMEM = pltpu.SMEM
VMEM = pltpu.VMEM
MESH = pl.DeviceIdType.MESH


def position():
    e = lax.axis_index("expert")
    return e // 8, (e // 2) % 4, e % 2


def plan_kernel(refit, placement, table, needed, where, slot_at, want, place):
    _, z, _ = position()
    experts, slots = refit.shape[0], placement.shape[0]
    for s in range(slots):
        where[placement[s]] = experts
    for p in range(experts):
        where[refit[p]] = p
    for k in range(3 * (experts + 1)):
        want[k] = 0
    for s in range(slots):
        row = (s // 4) % 4
        p = where[placement[s]]
        slot_at[s] = p
        want[p] = want[p] | (1 << row)
    counts = [jnp.int32(0)] * 4
    edge = jnp.logical_or(z == 0, z == 3)
    home = lax.select(z < 2, 0, 1)
    end = lax.select(z < 2, 0, 3)
    middle = lax.select(z < 2, 1, 2)
    for k in range(3 * 32):
        table[k] = 0
    for p in range(experts):
        row, lane = (p // 2) % 4, (p // 8) * 2 + p % 2
        half = row // 2
        mask = want[p]
        crosses = ((mask & (12 if half == 0 else 3)) != 0).astype(jnp.int32)
        to_end = [((mask & (1 << e)) != 0).astype(jnp.int32) if row != e else jnp.int32(0) for e in (0, 3)]
        mid_place = counts[half]
        end_place = lax.select(end == 0, counts[2], counts[3])
        here = lax.select(middle == row, lane, lax.select(home == half, 8 + lane, 16 + mid_place))
        mine = jnp.logical_and(crosses == 1, home == half)
        table[lax.select(mine, mid_place, 96)] = here
        goes = lax.select(end == 0, to_end[0], to_end[1])
        table[lax.select(goes == 1, 32 + end_place, 96)] = here
        place[p] = lax.select(z == row, lane, lax.select(edge, 16 + end_place, here))
        counts[half] = counts[half] + crosses
        counts[2] = counts[2] + to_end[0]
        counts[3] = counts[3] + to_end[1]
    place[experts] = ZERO
    for k in range(ROW_SLOTS):
        s = (k // 4) * 16 + z * 4 + k % 4
        table[64 + k] = place[slot_at[s]]
    needed[0] = jnp.maximum(jnp.maximum(counts[0], counts[1]), jnp.maximum(counts[2], counts[3]))


def make_plan(refit, placement):
    return pl.pallas_call(
        plan_kernel,
        out_shape=(jax.ShapeDtypeStruct((128,), jnp.int32), jax.ShapeDtypeStruct((1,), jnp.int32)),
        in_specs=[pl.BlockSpec(memory_space=SMEM)] * 2,
        out_specs=(pl.BlockSpec(memory_space=SMEM),) * 2,
        scratch_shapes=[SMEM((256,), jnp.int32), SMEM((64,), jnp.int32), SMEM((128,), jnp.int32), SMEM((40,), jnp.int32)],
        name="plan",
    )(refit, placement)


def place_kernel(capacity, steps, table, prior, left, right, out, sib, own, row, far, near, mids, ends, pair, final, work,
                 sib_in, row_in, far_in, near_in, pair_in, out_in, sent):
    x, z, c = position()
    t_axis = lax.axis_index("tensor")
    size = CHUNK
    width = prior.shape[2]
    block = prior.shape[1] // COLUMNS
    edge = jnp.logical_or(z == 0, z == 3)
    middle = jnp.logical_not(edge)
    along = lax.select(z < 2, 1 - z, 5 - z)
    across = lax.select(z == 1, 2, 1)

    def at(x_, z_, c_):
        return (x_ * 8 + z_ * 2 + c_, t_axis)

    sibling = at(x, z, 1 - c)
    inward = at(x, along, c)
    other = at(x, lax.select(edge, along, across), c)

    def remote(src, dst, send, recv, to):
        return pltpu.make_async_remote_copy(src_ref=src, dst_ref=dst, send_sem=sent.at[send], recv_sem=recv, device_id=to, device_id_type=MESH)

    def compute(t):
        for g in range(COLUMNS):
            for mine in (True, False):
                half = c if mine else 1 - c
                start = pl.multiple_of(g * block + t * (2 * size) + half * size, size)
                rows = pl.ds(start, size)
                update = jnp.dot(left[0, rows, :], right[0], preferred_element_type=jnp.float32)
                merged = (prior[0, rows, :].astype(jnp.float32) + SCALE * update).astype(jnp.bfloat16)
                if mine:
                    own[t, g, c] = merged
                else:
                    sib[t, g] = merged
        remote(sib.at[t], own.at[t, :, c], 0, sib_in.at[t], sibling).start()

    def scatter(t):
        remote(sib.at[t], own.at[t, :, 1 - c], 0, sib_in.at[t], sibling).wait_recv()
        for d in (2, 1, 3):
            to = (x + d) % COLUMNS
            remote(own.at[t, to], row.at[t, pl.ds(2 * x, 2)], 1, row_in.at[t], at(to, z, c)).start()
        row[t, pl.ds(2 * x, 2)] = own[t, x]

    def row_arrived(t):
        remote(row.at[t, pl.ds(0, 6)], row.at[t, pl.ds(0, 6)], 1, row_in.at[t], sibling).wait_recv()

    def edge_send(t):
        row_arrived(t)
        remote(row.at[t], far.at[t], 2, far_in.at[t], inward).start()

    def pick_mid(t):
        row_arrived(t)
        remote(row.at[t], far.at[t], 2, far_in.at[t], inward).wait_recv()
        w = t % RING
        work[w, 0:8] = row[t]
        work[w, 8:16] = far[t]
        for k in range(capacity):
            mids[t, k] = work[w, table[k]]
        remote(mids.at[t], near.at[t], 3, near_in.at[t], other).start()

    def pick_slots(t):
        w = t % RING
        for k in range(ROW_SLOTS):
            g, core, j = k // 4, (k // 2) % 2, k % 2
            half = c if core == 0 else 1 - c
            piece = work[w, table[64 + g * 4 + half * 2 + j]]
            if core == 0:
                final[t, g, j, pl.ds(pl.multiple_of(c * size, size), size)] = piece
            else:
                pair[t, g, j] = piece
        remote(pair.at[t], final.at[t, :, :, pl.ds(pl.multiple_of(c * size, size), size)], 5, pair_in.at[t], sibling).start()

    def near_arrived(t):
        remote(near.at[t], near.at[t], 3, near_in.at[t], other).wait_recv()
        work[t % RING, 16:16 + capacity] = near[t]

    def finish_middle(t):
        near_arrived(t)
        w = t % RING
        for k in range(capacity):
            ends[t, k] = work[w, table[32 + k]]
        remote(ends.at[t], near.at[t], 4, near_in.at[t], inward).start()
        pick_slots(t)

    def finish_edge(t):
        near_arrived(t)
        work[t % RING, 0:8] = row[t]
        pick_slots(t)

    def deliver(t):
        remote(pair.at[t], pair.at[t], 5, pair_in.at[t], sibling).wait_recv()
        rows = pl.ds(pl.multiple_of(x * block + t * (2 * size), 2 * size), 2 * size)
        for d in (2, 1, 3):
            to = (x + d) % COLUMNS
            remote(final.at[t, to], out.at[:, rows], 6, out_in.at[0], at(to, z, c)).start()
        pltpu.make_async_copy(final.at[t, x], out.at[:, rows], out_in.at[1]).start()

    barrier = pltpu.get_barrier_semaphore()
    for peer in (sibling, inward, at((x + 1) % 4, z, c), at((x + 2) % 4, z, c), at((x + 3) % 4, z, c)):
        pl.semaphore_signal(barrier, inc=1, device_id=peer, device_id_type=MESH)

    @pl.when(middle)
    def _():
        pl.semaphore_signal(barrier, inc=1, device_id=other, device_id_type=MESH)

    for w in range(RING):
        work[w, ZERO] = jnp.zeros((size, width), jnp.bfloat16)
    pl.semaphore_wait(barrier, lax.select(middle, 6, 5))

    def stage(i, delay, body, role=None):
        t = i - delay
        live = jnp.logical_and(t >= 0, t < steps)

        @pl.when(live if role is None else jnp.logical_and(live, role))
        def _():
            body(t)

    last = 8

    @pl.loop(0, steps + last)
    def _(i):
        stage(i, 0, compute)
        stage(i, 1, scatter)
        stage(i, 3, edge_send, edge)
        stage(i, 4, pick_mid, middle)
        stage(i, 5, finish_middle, middle)
        stage(i, 7, finish_edge, edge)
        stage(i, 6, deliver, middle)
        stage(i, 8, deliver, edge)

    remote(sib, sib, 0, sib_in.at[0], sibling).wait_send()
    remote(own.at[:, 0:3], own.at[:, 0:3], 1, sib_in.at[0], sibling).wait_send()

    @pl.when(edge)
    def _():
        remote(row, row, 2, sib_in.at[0], sibling).wait_send()

    @pl.when(middle)
    def _():
        remote(mids, mids, 3, sib_in.at[0], sibling).wait_send()
        remote(ends, ends, 4, sib_in.at[0], sibling).wait_send()

    remote(pair, pair, 5, sib_in.at[0], sibling).wait_send()
    remote(final.at[:, 0:3], final.at[:, 0:3], 6, sib_in.at[0], sibling).wait_send()
    most = out.at[:, pl.ds(0, 3 * block)]
    remote(most, most, 6, out_in.at[0], sibling).wait_recv()
    rest = out.at[:, pl.ds(0, block)]
    pltpu.make_async_copy(rest, rest, out_in.at[1]).wait()


def place(capacity, number, table, prior, left, right):
    _, depth, width = prior.shape
    size = CHUNK
    steps = depth // (ROW_EXPERTS * size)
    dtype = jnp.bfloat16

    def buffer(*shape):
        return VMEM(shape + (width,), dtype)

    vmem = pl.BlockSpec(memory_space=VMEM)
    return pl.pallas_call(
        functools.partial(place_kernel, capacity, steps),
        out_shape=jax.ShapeDtypeStruct((2, depth, width), dtype),
        in_specs=[pl.BlockSpec(memory_space=SMEM), vmem, vmem, vmem],
        out_specs=pl.BlockSpec(memory_space=pl.ANY),
        scratch_shapes=[
            buffer(steps, COLUMNS, size),
            buffer(steps, COLUMNS, 2, size),
            buffer(steps, ROW_EXPERTS, size),
            buffer(steps, ROW_EXPERTS, size),
            buffer(steps, capacity, size),
            buffer(steps, capacity, size),
            buffer(steps, capacity, size),
            buffer(steps, COLUMNS, 2, size),
            buffer(steps, COLUMNS, 2, 2 * size),
            buffer(RING, ZERO + 1, size),
            pltpu.SemaphoreType.DMA((steps,)),
            pltpu.SemaphoreType.DMA((steps,)),
            pltpu.SemaphoreType.DMA((steps,)),
            pltpu.SemaphoreType.DMA((steps,)),
            pltpu.SemaphoreType.DMA((steps,)),
            pltpu.SemaphoreType.DMA((2,)),
            pltpu.SemaphoreType.DMA((7,)),
        ],
        compiler_params=pltpu.CompilerParams(collective_id=number, has_side_effects=True, vmem_limit_bytes=62 << 20),
        name="place%d" % capacity,
    )(table, prior, left, right)


def per_device(prior_gate_weight, left_factor, right_factor, refit_expert_index, placement):
    table, needed = make_plan(refit_expert_index, placement)
    operands = (table, prior_gate_weight, left_factor, right_factor)
    if len(CAPACITIES) == 1:
        return place(CAPACITIES[0], 0, *operands)
    branch = sum((needed[0] > capacity).astype(jnp.int32) for capacity in CAPACITIES[:-1])
    branches = [functools.partial(place, capacity, n) for n, capacity in enumerate(CAPACITIES)]
    return lax.switch(branch, branches, *operands)


def solution(mesh):
    return jax.shard_map(
        per_device,
        mesh=mesh,
        in_specs=(
            P("expert", None, "tensor"),
            P("expert", None, None),
            P("expert", None, "tensor"),
            P(),
            P(),
        ),
        out_specs=P("expert", None, "tensor"),
        check_vma=False,
    )
```

time: 442 us -> 205 us (0.46)
  blocking collectives: 261 us -> 0 us
  Pallas kernels: 0 us -> 196 us
  local copies, waits for them, and re-layouts: 131 us -> 9.19 us
  other arithmetic: 38.3 us -> 0 us
  matrix products: 10.4 us -> 0 us
    all_to_all x2 -> x0, blocking collectives: 261 us -> none  [the longest x1 166 us: per_device(): lax.all_to_all(picked, 'expert', split_axis=0, concat_axis=1, tiled=True)]
    pallas_call x0 -> x2, Pallas kernels: none -> 196 us  [the longest x1 194 us: place(): pl.pallas_call(functools.partial(place_kernel, capacity, steps), out_shap...]
    all_to_all x2 -> x0, local copies, waits for them, and re-layouts: 48.1 us -> none  [the longest x1 41.4 us: per_device(): lax.all_to_all(merged_gate, 'expert', split_axis=1, concat_axis=0, tiled=...]
    convert_element_type x1 -> x0, local copies, waits for them, and re-layouts: 43.4 us -> none  [merge_expert_block(): (gate_weight.astype(jnp.float32) + update_scale * lowrank_update).astype(...]
    unnamed x1 -> x0, other arithmetic: 38.3 us -> none
    unnamed x12 -> x2, local copies, waits for them, and re-layouts: 34.3 us -> 9.19 us
    dot_general x2 -> x0, matrix products: 10.4 us -> none  [the longest x1 7.19 us: per_device(): jnp.dot(selector, flattened, preferred_element_type=jnp.float32)]
    reshape x1 -> x0, local copies, waits for them, and re-layouts: 5.25 us -> none  [per_device(): flattened = row_block.reshape(refit_count, depth * width)]
where the time goes in v1:
time: 205 us
  Pallas kernels  196 us (96%)
  local copies, waits for them, and re-layouts  9.19 us (4%)
    pallas_call x1, Pallas kernels, place(): pl.pallas_call(functools.partial(place_kernel, capacity, steps), out_shap...  194 us
    unnamed x2, local copies, waits for them, and re-layouts  9.19 us

profile of v1, /device:TPU:1, one launch (start us, length us, event | category | flops | bytes accessed | tf_op | source)
XLA Modules:
  0.0 204.9 jit_solution(2722293142017467919)
XLA Ops:
  0.0 1.9 plan.1
  1.9 2.6 %copy.6.left = bf16[1,7168,64]{2,1,0:T(8,128)(2,1)} copy(bf16[1,7168,64]{1,2,0:T(8,128)(2,1)} %param.6) | data formatting | bytes 1835008 | tf_op args[1]
  4.5 193.8 %place16.1 = bf16[2,7168,256]{2,1,0:T(8,128)(2,1)} custom-call(s32[128]{0:T(128)} %get-tuple-element.6.table, bf16[1,7168,256]{2,1,0:T(8,128)(2,1)} %prior.1, bf16[1,7168,64]{2,1,0:T(8,128)(2,1)} %copy.6.left, bf16[1,64,256]{2,1,0:T(8,128)(2,1)} %right.1), custom_call_target="tpu_custom_call" | custom-call | tf_op jit(solution)/shard_map/place16/pallas_call | solution.py:245
  198.3 6.6 %copy.8 = bf16[2,7168,256]{2,1,0:T(8,128)(2,1)} copy(bf16[2,7168,256]{2,1,0:T(8,128)(2,1)} %place16.1) | data formatting | bytes 14680064

commit v2 on v1

--- a/solution.py
+++ b/solution.py
@@ -13,9 +13,14 @@
 ROW_EXPERTS = 8
 ROW_SLOTS = 16
 CHUNK = 32
-CAPACITIES = (16,)
+CAPACITIES = (10, 11, 12, 13, 14, 16)
 ZERO = 32
 RING = 4
+EDGE_SEND = 2
+PICK_MID = 3
+FINISH_MIDDLE = 4
+FINISH_EDGE = 6
+LAST = FINISH_EDGE + 1
 SMEM = pltpu.SMEM
 VMEM = pltpu.VMEM
 MESH = pl.DeviceIdType.MESH
@@ -104,26 +109,27 @@
     def remote(src, dst, send, recv, to):
         return pltpu.make_async_remote_copy(src_ref=src, dst_ref=dst, send_sem=sent.at[send], recv_sem=recv, device_id=to, device_id_type=MESH)
 
-    def compute(t):
+    def compute(i):
         for g in range(COLUMNS):
-            for mine in (True, False):
-                half = c if mine else 1 - c
-                start = pl.multiple_of(g * block + t * (2 * size) + half * size, size)
-                rows = pl.ds(start, size)
-                update = jnp.dot(left[0, rows, :], right[0], preferred_element_type=jnp.float32)
-                merged = (prior[0, rows, :].astype(jnp.float32) + SCALE * update).astype(jnp.bfloat16)
-                if mine:
-                    own[t, g, c] = merged
-                else:
-                    sib[t, g] = merged
-        remote(sib.at[t], own.at[t, :, c], 0, sib_in.at[t], sibling).start()
-
-    def scatter(t):
-        remote(sib.at[t], own.at[t, :, 1 - c], 0, sib_in.at[t], sibling).wait_recv()
-        for d in (2, 1, 3):
-            to = (x + d) % COLUMNS
-            remote(own.at[t, to], row.at[t, pl.ds(2 * x, 2)], 1, row_in.at[t], at(to, z, c)).start()
-        row[t, pl.ds(2 * x, 2)] = own[t, x]
+            rows = pl.ds(pl.multiple_of(g * block + i * (4 * size), 4 * size), 4 * size)
+            update = lax.dot_general(left[0, :, rows], right[0], (((0,), (0,)), ((), ())), preferred_element_type=jnp.float32)
+            merged = (prior[0, rows, :].astype(jnp.float32) + SCALE * update).astype(jnp.bfloat16)
+            for n in range(2):
+                first, second = (merged[(2 * n + m) * size:(2 * n + m + 1) * size] for m in range(2))
+                own[2 * i + n, g, c] = jnp.where(c == 0, first, second)
+                sib[2 * i + n, g] = jnp.where(c == 0, second, first)
+        for n in range(2):
+            t = 2 * i + n
+            remote(sib.at[t], own.at[t, :, c], 0, sib_in.at[t], sibling).start()
+
+    def scatter(i):
+        for n in range(2):
+            t = 2 * i + n
+            remote(sib.at[t], own.at[t, :, 1 - c], 0, sib_in.at[t], sibling).wait_recv()
+            for d in (2, 1, 3):
+                to = (x + d) % COLUMNS
+                remote(own.at[t, to], row.at[t, pl.ds(2 * x, 2)], 1, row_in.at[t], at(to, z, c)).start()
+            row[t, pl.ds(2 * x, 2)] = own[t, x]
 
     def row_arrived(t):
         remote(row.at[t, pl.ds(0, 6)], row.at[t, pl.ds(0, 6)], 1, row_in.at[t], sibling).wait_recv()
@@ -191,26 +197,24 @@
         work[w, ZERO] = jnp.zeros((size, width), jnp.bfloat16)
     pl.semaphore_wait(barrier, lax.select(middle, 6, 5))
 
-    def stage(i, delay, body, role=None):
+    def stage(i, delay, count, body, role=None):
         t = i - delay
-        live = jnp.logical_and(t >= 0, t < steps)
+        live = jnp.logical_and(t >= 0, t < count)
 
         @pl.when(live if role is None else jnp.logical_and(live, role))
         def _():
             body(t)
 
-    last = 8
-
-    @pl.loop(0, steps + last)
+    @pl.loop(0, steps + LAST)
     def _(i):
-        stage(i, 0, compute)
-        stage(i, 1, scatter)
-        stage(i, 3, edge_send, edge)
-        stage(i, 4, pick_mid, middle)
-        stage(i, 5, finish_middle, middle)
-        stage(i, 7, finish_edge, edge)
-        stage(i, 6, deliver, middle)
-        stage(i, 8, deliver, edge)
+        stage(i, 0, steps // 2, compute)
+        stage(i, 1, steps // 2, scatter)
+        stage(i, EDGE_SEND, steps, edge_send, edge)
+        stage(i, PICK_MID, steps, pick_mid, middle)
+        stage(i, FINISH_MIDDLE, steps, finish_middle, middle)
+        stage(i, FINISH_EDGE, steps, finish_edge, edge)
+        stage(i, FINISH_MIDDLE + 1, steps, deliver, middle)
+        stage(i, FINISH_EDGE + 1, steps, deliver, edge)
 
     remote(sib, sib, 0, sib_in.at[0], sibling).wait_send()
     remote(own.at[:, 0:3], own.at[:, 0:3], 1, sib_in.at[0], sibling).wait_send()
@@ -273,7 +277,7 @@
 
 def per_device(prior_gate_weight, left_factor, right_factor, refit_expert_index, placement):
     table, needed = make_plan(refit_expert_index, placement)
-    operands = (table, prior_gate_weight, left_factor, right_factor)
+    operands = (table, prior_gate_weight, jnp.swapaxes(left_factor, 1, 2), right_factor)
     if len(CAPACITIES) == 1:
         return place(CAPACITIES[0], 0, *operands)
     branch = sum((needed[0] > capacity).astype(jnp.int32) for capacity in CAPACITIES[:-1])

time: 205 us -> 166 us (0.81)
  Pallas kernels: 196 us -> 156 us
  between operations: 0.02 us -> 3.26 us
  local copies, waits for them, and re-layouts: 9.19 us -> 6.6 us
    pallas_call x1, Pallas kernels: 194 us -> 154 us  [place(): pl.pallas_call(functools.partial(place_kernel, capacity, steps), out_shap...]
    unnamed x2 -> x1, local copies, waits for them, and re-layouts: 9.19 us -> 6.6 us
where the time goes in v2:
time: 166 us
  Pallas kernels  156 us (94%)
  local copies, waits for them, and re-layouts  6.6 us (4%)
  between operations  3.26 us (2%)
    pallas_call x1, Pallas kernels, place(): pl.pallas_call(functools.partial(place_kernel, capacity, steps), out_shap...  154 us
    unnamed x1, local copies, waits for them, and re-layouts  6.6 us

profile of v2, /device:TPU:1, one launch (start us, length us, event | category | flops | bytes accessed | tf_op | source)
XLA Modules:
  0.0 165.6 jit_solution(5593880971589235409)
XLA Ops:
  0.0 2.0 %plan.1 = (s32[128]{0:T(128)S(1)}, s32[1]{0:T(128)}) custom-call(s32[32]{0:T(128)} %refit.1, s32[64]{0:T(128)} %placement.1), custom_call_target="tpu_custom_call" | custom-call | tf_op jit(solution)/shard_map/plan/pallas_call | solution.py:80
  5.2 153.7 %conditional.1 = (bf16[2,7168,256]{2,1,0:T(8,128)(2,1)}) conditional(s32[]{:T(128)} %bitcast, (s32[128]{0:T(128)S(1)}, bf16[1,7168,256]{2,1,0:T(8,128)(2,1)}, bf16[1,64,7168]{2,1,0:T(8,128)(2,1)}, bf16[1,64,256]{2,1,0:T(8,128)(2,1)}) %tuple.36, (s32[128]{0:T(128)S(1)}, bf16[1,7168,256]{2,1,0:T(8,128)(2,1)}, ...), branch_computations={%region_0.0_spmd, %region_1.0_spmd, %region_2.0_spmd, %region_3.0_... | conditional | bytes 8 | solution.py:285
  5.3 153.7 %place12.1 = bf16[2,7168,256]{2,1,0:T(8,128)(2,1)} custom-call(s32[128]{0:T(128)S(1)} %get-tuple-element.68.table, bf16[1,7168,256]{2,1,0:T(8,128)(2,1)} %get-tuple-element.103.prior, bf16[1,64,7168]{2,1,0:T(8,128)(2,1)} %get-tuple-element.70.left, bf16[1,64,256]{2,1,0:T(8,128)(2,1)} %get-tuple-element.109.right), custom_call_target="tpu_custom_call" | custom-call | tf_op jit(solution)/shard_map/cond/branch_2_fun/place12/pallas_call | solution.py:249
  159.0 6.6 %copy.31 = bf16[2,7168,256]{2,1,0:T(8,128)(2,1)} copy(bf16[2,7168,256]{2,1,0:T(8,128)(2,1)} %get-tuple-element.88) | data formatting | bytes 14680064

commit v3 on v2

--- a/solution.py
+++ b/solution.py
@@ -12,14 +12,15 @@
 ROWS = 4
 ROW_EXPERTS = 8
 ROW_SLOTS = 16
-CHUNK = 32
+CHUNK = 16
 CAPACITIES = (10, 11, 12, 13, 14, 16)
 ZERO = 32
-RING = 4
+RING = 8
+GROUP = 8
 EDGE_SEND = 2
-PICK_MID = 3
-FINISH_MIDDLE = 4
-FINISH_EDGE = 6
+PICK_MID = 4
+FINISH_MIDDLE = 8
+FINISH_EDGE = 12
 LAST = FINISH_EDGE + 1
 SMEM = pltpu.SMEM
 VMEM = pltpu.VMEM
@@ -92,6 +93,7 @@
     x, z, c = position()
     t_axis = lax.axis_index("tensor")
     size = CHUNK
+    front = 128 // (2 * size)
     width = prior.shape[2]
     block = prior.shape[1] // COLUMNS
     edge = jnp.logical_or(z == 0, z == 3)
@@ -111,20 +113,20 @@
 
     def compute(i):
         for g in range(COLUMNS):
-            rows = pl.ds(pl.multiple_of(g * block + i * (4 * size), 4 * size), 4 * size)
+            rows = pl.ds(pl.multiple_of(g * block + i * 128, 128), 128)
             update = lax.dot_general(left[0, :, rows], right[0], (((0,), (0,)), ((), ())), preferred_element_type=jnp.float32)
             merged = (prior[0, rows, :].astype(jnp.float32) + SCALE * update).astype(jnp.bfloat16)
-            for n in range(2):
+            for n in range(front):
                 first, second = (merged[(2 * n + m) * size:(2 * n + m + 1) * size] for m in range(2))
-                own[2 * i + n, g, c] = jnp.where(c == 0, first, second)
-                sib[2 * i + n, g] = jnp.where(c == 0, second, first)
-        for n in range(2):
-            t = 2 * i + n
+                own[front * i + n, g, c] = jnp.where(c == 0, first, second)
+                sib[front * i + n, g] = jnp.where(c == 0, second, first)
+        for n in range(front):
+            t = front * i + n
             remote(sib.at[t], own.at[t, :, c], 0, sib_in.at[t], sibling).start()
 
     def scatter(i):
-        for n in range(2):
-            t = 2 * i + n
+        for n in range(front):
+            t = front * i + n
             remote(sib.at[t], own.at[t, :, 1 - c], 0, sib_in.at[t], sibling).wait_recv()
             for d in (2, 1, 3):
                 to = (x + d) % COLUMNS
@@ -137,6 +139,13 @@
     def edge_send(t):
         row_arrived(t)
         remote(row.at[t], far.at[t], 2, far_in.at[t], inward).start()
+
+    def pick(w, to, t, start):
+        for low in range(0, capacity, GROUP):
+            spots = range(low, min(low + GROUP, capacity))
+            pieces = [work[w, table[start + k]] for k in spots]
+            for k, piece in zip(spots, pieces):
+                to[t, k] = piece
 
     def pick_mid(t):
         row_arrived(t)
@@ -144,21 +153,23 @@
         w = t % RING
         work[w, 0:8] = row[t]
         work[w, 8:16] = far[t]
-        for k in range(capacity):
-            mids[t, k] = work[w, table[k]]
+        pick(w, mids, t, 0)
         remote(mids.at[t], near.at[t], 3, near_in.at[t], other).start()
 
     def pick_slots(t):
         w = t % RING
-        for k in range(ROW_SLOTS):
-            g, core, j = k // 4, (k // 2) % 2, k % 2
+        mine = pl.ds(pl.multiple_of(c * size, size), size)
+        for core in range(2):
             half = c if core == 0 else 1 - c
-            piece = work[w, table[64 + g * 4 + half * 2 + j]]
-            if core == 0:
-                final[t, g, j, pl.ds(pl.multiple_of(c * size, size), size)] = piece
-            else:
-                pair[t, g, j] = piece
-        remote(pair.at[t], final.at[t, :, :, pl.ds(pl.multiple_of(c * size, size), size)], 5, pair_in.at[t], sibling).start()
+            for low in range(0, COLUMNS, GROUP // 2):
+                spots = [(g, j) for g in range(low, min(low + GROUP // 2, COLUMNS)) for j in range(2)]
+                pieces = [work[w, table[64 + g * 4 + half * 2 + j]] for g, j in spots]
+                for (g, j), piece in zip(spots, pieces):
+                    if core == 0:
+                        final[t, g, j, mine] = piece
+                    else:
+                        pair[t, g, j] = piece
+        remote(pair.at[t], final.at[t, :, :, mine], 5, pair_in.at[t], sibling).start()
 
     def near_arrived(t):
         remote(near.at[t], near.at[t], 3, near_in.at[t], other).wait_recv()
@@ -167,8 +178,7 @@
     def finish_middle(t):
         near_arrived(t)
         w = t % RING
-        for k in range(capacity):
-            ends[t, k] = work[w, table[32 + k]]
+        pick(w, ends, t, 32)
         remote(ends.at[t], near.at[t], 4, near_in.at[t], inward).start()
         pick_slots(t)
 
@@ -207,8 +217,8 @@
 
     @pl.loop(0, steps + LAST)
     def _(i):
-        stage(i, 0, steps // 2, compute)
-        stage(i, 1, steps // 2, scatter)
+        stage(i, 0, steps // front, compute)
+        stage(i, 1, steps // front, scatter)
         stage(i, EDGE_SEND, steps, edge_send, edge)
         stage(i, PICK_MID, steps, pick_mid, middle)
         stage(i, FINISH_MIDDLE, steps, finish_middle, middle)
@@ -248,9 +258,9 @@
     vmem = pl.BlockSpec(memory_space=VMEM)
     return pl.pallas_call(
         functools.partial(place_kernel, capacity, steps),
-        out_shape=jax.ShapeDtypeStruct((2, depth, width), dtype),
+        out_shape=VMEM((2, depth, width), dtype),
         in_specs=[pl.BlockSpec(memory_space=SMEM), vmem, vmem, vmem],
-        out_specs=pl.BlockSpec(memory_space=pl.ANY),
+        out_specs=vmem,
         scratch_shapes=[
             buffer(steps, COLUMNS, size),
             buffer(steps, COLUMNS, 2, size),
@@ -270,7 +280,7 @@
             pltpu.SemaphoreType.DMA((2,)),
             pltpu.SemaphoreType.DMA((7,)),
         ],
-        compiler_params=pltpu.CompilerParams(collective_id=number, has_side_effects=True, vmem_limit_bytes=62 << 20),
+        compiler_params=pltpu.CompilerParams(collective_id=number, has_side_effects=True, vmem_limit_bytes=52 << 20),
         name="place%d" % capacity,
     )(table, prior, left, right)
 

time: 166 us -> 158 us (0.952)
  Pallas kernels: 156 us -> 151 us
  local copies, waits for them, and re-layouts: 6.6 us -> 3.05 us
    pallas_call x1, Pallas kernels: 154 us -> 149 us  [place(): pl.pallas_call(functools.partial(place_kernel, capacity, steps), out_shap...]
    unnamed x1, local copies, waits for them, and re-layouts: 6.6 us -> 3.05 us
where the time goes in v3:
time: 158 us; the launch traced here: 157 us
  Pallas kernels  151 us (96%)
  between operations  3.26 us (2%)
  local copies, waits for them, and re-layouts  3.05 us (2%)
    pallas_call x1, Pallas kernels, place(): pl.pallas_call(functools.partial(place_kernel, capacity, steps), out_shap...  149 us

profile of v3, /device:TPU:1, one launch (start us, length us, event | category | flops | bytes accessed | tf_op | source)
XLA Modules:
  0.0 157.4 jit_solution(2951405129198123599)
XLA Ops:
  0.0 2.0 %plan.1 = (s32[128]{0:T(128)S(1)}, s32[1]{0:T(128)}) custom-call(s32[32]{0:T(128)} %refit.1, s32[64]{0:T(128)} %placement.1), custom_call_target="tpu_custom_call" | custom-call | tf_op jit(solution)/shard_map/plan/pallas_call | solution.py:81
  5.2 149.1 %conditional.1 = (bf16[2,7168,256]{2,1,0:T(8,128)(2,1)S(1)}) conditional(s32[]{:T(128)} %bitcast, (s32[128]{0:T(128)S(1)}, bf16[1,7168,256]{2,1,0:T(8,128)(2,1)}, bf16[1,64,7168]{2,1,0:T(8,128)(2,1)}, bf16[1,64,256]{2,1,0:T(8,128)(2,1)}) %tuple.36, (s32[128]{0:T(128)S(1)}, bf16[1,7168,256]{2,1,0:T(8,128)(2,1)}, ...), branch_computations={%region_0.0_spmd, %region_1.0_spmd, %region_2.0_spmd, %region_3.0_... | conditional | bytes 8 | solution.py:295
  5.3 149.1 %place12.1 = bf16[2,7168,256]{2,1,0:T(8,128)(2,1)S(1)} custom-call(s32[128]{0:T(128)S(1)} %get-tuple-element.68.table, bf16[1,7168,256]{2,1,0:T(8,128)(2,1)} %get-tuple-element.103.prior, bf16[1,64,7168]{2,1,0:T(8,128)(2,1)} %get-tuple-element.70.left, bf16[1,64,256]{2,1,0:T(8,128)(2,1)} %get-tuple-element.109.right), custom_call_target="tpu_custom_call" | custom-call | tf_op jit(solution)/shard_map/cond/branch_2_fun/place12/pallas_call | solution.py:259
  154.4 3.1 %copy.31 = bf16[2,7168,256]{2,1,0:T(8,128)(2,1)} copy(bf16[2,7168,256]{2,1,0:T(8,128)(2,1)S(1)} %get-tuple-element.88) | data formatting | bytes 14680064

commit v4 on v3

--- a/solution.py
+++ b/solution.py
@@ -17,10 +17,10 @@
 ZERO = 32
 RING = 8
 GROUP = 8
-EDGE_SEND = 2
+EDGE_SEND = 3
 PICK_MID = 4
-FINISH_MIDDLE = 8
-FINISH_EDGE = 12
+FINISH_MIDDLE = 7
+FINISH_EDGE = 10
 LAST = FINISH_EDGE + 1
 SMEM = pltpu.SMEM
 VMEM = pltpu.VMEM
@@ -32,7 +32,7 @@
     return e // 8, (e // 2) % 4, e % 2
 
 
-def plan_kernel(refit, placement, table, needed, where, slot_at, want, place):
+def plan_kernel(refit, placement, table, branch, where, slot_at, want, place):
     _, z, _ = position()
     experts, slots = refit.shape[0], placement.shape[0]
     for s in range(slots):
@@ -74,7 +74,8 @@
     for k in range(ROW_SLOTS):
         s = (k // 4) * 16 + z * 4 + k % 4
         table[64 + k] = place[slot_at[s]]
-    needed[0] = jnp.maximum(jnp.maximum(counts[0], counts[1]), jnp.maximum(counts[2], counts[3]))
+    most = jnp.maximum(jnp.maximum(counts[0], counts[1]), jnp.maximum(counts[2], counts[3]))
+    branch[0] = sum((most > capacity).astype(jnp.int32) for capacity in CAPACITIES[:-1]) + jnp.int32(0)
 
 
 def make_plan(refit, placement):
@@ -88,14 +89,14 @@
     )(refit, placement)
 
 
-def place_kernel(capacity, steps, table, prior, left, right, out, sib, own, row, far, near, mids, ends, pair, final, work,
-                 sib_in, row_in, far_in, near_in, pair_in, out_in, sent):
+def place_kernel(capacity, steps, table, prior_all, left_all, right_all, out, prior, left, right, sib, own, row, far, near, mids, ends, pair, final, work,
+                 sib_in, row_in, far_in, near_in, pair_in, out_in, sent, fetched):
     x, z, c = position()
     t_axis = lax.axis_index("tensor")
     size = CHUNK
     front = 128 // (2 * size)
     width = prior.shape[2]
-    block = prior.shape[1] // COLUMNS
+    block = prior.shape[1]
     edge = jnp.logical_or(z == 0, z == 3)
     middle = jnp.logical_not(edge)
     along = lax.select(z < 2, 1 - z, 5 - z)
@@ -112,21 +113,27 @@
         return pltpu.make_async_remote_copy(src_ref=src, dst_ref=dst, send_sem=sent.at[send], recv_sem=recv, device_id=to, device_id_type=MESH)
 
     def compute(i):
-        for g in range(COLUMNS):
-            rows = pl.ds(pl.multiple_of(g * block + i * 128, 128), 128)
+        part = i // 2
+        for k in range(COLUMNS // 2):
+            g = (i % 2) * (COLUMNS // 2) + k
+            start = part * 128
+            rows = pl.ds(pl.multiple_of(g * block + start, 128), 128)
             update = lax.dot_general(left[0, :, rows], right[0], (((0,), (0,)), ((), ())), preferred_element_type=jnp.float32)
-            merged = (prior[0, rows, :].astype(jnp.float32) + SCALE * update).astype(jnp.bfloat16)
+            merged = (prior[g, pl.ds(pl.multiple_of(start, 128), 128), :].astype(jnp.float32) + SCALE * update).astype(jnp.bfloat16)
             for n in range(front):
                 first, second = (merged[(2 * n + m) * size:(2 * n + m + 1) * size] for m in range(2))
-                own[front * i + n, g, c] = jnp.where(c == 0, first, second)
-                sib[front * i + n, g] = jnp.where(c == 0, second, first)
-        for n in range(front):
-            t = front * i + n
-            remote(sib.at[t], own.at[t, :, c], 0, sib_in.at[t], sibling).start()
+                own[front * part + n, g, c] = jnp.where(c == 0, first, second)
+                sib[front * part + n, g] = jnp.where(c == 0, second, first)
+
+        @pl.when(i % 2 == 1)
+        def _():
+            for n in range(front):
+                t = front * part + n
+                remote(sib.at[t], own.at[t, :, c], 0, sib_in.at[t], sibling).start()
 
     def scatter(i):
-        for n in range(front):
-            t = front * i + n
+        for n in range(front // 2):
+            t = front // 2 * i + n
             remote(sib.at[t], own.at[t, :, 1 - c], 0, sib_in.at[t], sibling).wait_recv()
             for d in (2, 1, 3):
                 to = (x + d) % COLUMNS
@@ -195,6 +202,15 @@
             remote(final.at[t, to], out.at[:, rows], 6, out_in.at[0], at(to, z, c)).start()
         pltpu.make_async_copy(final.at[t, x], out.at[:, rows], out_in.at[1]).start()
 
+    early, late = pl.ds(0, 128), pl.ds(128, block - 128)
+    fetches = [
+        pltpu.make_async_copy(right_all, right, fetched.at[0]),
+        pltpu.make_async_copy(prior_all.at[:, early], prior.at[:, early], fetched.at[1]),
+        pltpu.make_async_copy(left_all, left, fetched.at[2]),
+        pltpu.make_async_copy(prior_all.at[:, late], prior.at[:, late], fetched.at[3]),
+    ]
+    for fetch in fetches:
+        fetch.start()
     barrier = pltpu.get_barrier_semaphore()
     for peer in (sibling, inward, at((x + 1) % 4, z, c), at((x + 2) % 4, z, c), at((x + 3) % 4, z, c)):
         pl.semaphore_signal(barrier, inc=1, device_id=peer, device_id_type=MESH)
@@ -205,6 +221,8 @@
 
     for w in range(RING):
         work[w, ZERO] = jnp.zeros((size, width), jnp.bfloat16)
+    for fetch in fetches[:3]:
+        fetch.wait()
     pl.semaphore_wait(barrier, lax.select(middle, 6, 5))
 
     def stage(i, delay, count, body, role=None):
@@ -217,8 +235,12 @@
 
     @pl.loop(0, steps + LAST)
     def _(i):
-        stage(i, 0, steps // front, compute)
-        stage(i, 1, steps // front, scatter)
+        @pl.when(i == 2)
+        def _():
+            fetches[3].wait()
+
+        stage(i, 0, 2 * steps // front, compute)
+        stage(i, 2, 2 * steps // front, scatter)
         stage(i, EDGE_SEND, steps, edge_send, edge)
         stage(i, PICK_MID, steps, pick_mid, middle)
         stage(i, FINISH_MIDDLE, steps, finish_middle, middle)
@@ -248,6 +270,7 @@
 
 def place(capacity, number, table, prior, left, right):
     _, depth, width = prior.shape
+    prior = prior.reshape(COLUMNS, depth // COLUMNS, width)
     size = CHUNK
     steps = depth // (ROW_EXPERTS * size)
     dtype = jnp.bfloat16
@@ -259,9 +282,12 @@
     return pl.pallas_call(
         functools.partial(place_kernel, capacity, steps),
         out_shape=VMEM((2, depth, width), dtype),
-        in_specs=[pl.BlockSpec(memory_space=SMEM), vmem, vmem, vmem],
+        in_specs=[pl.BlockSpec(memory_space=SMEM)] + [pl.BlockSpec(memory_space=pl.ANY)] * 3,
         out_specs=vmem,
         scratch_shapes=[
+            VMEM(prior.shape, dtype),
+            VMEM(left.shape, dtype),
+            VMEM(right.shape, dtype),
             buffer(steps, COLUMNS, size),
             buffer(steps, COLUMNS, 2, size),
             buffer(steps, ROW_EXPERTS, size),
@@ -279,6 +305,7 @@
             pltpu.SemaphoreType.DMA((steps,)),
             pltpu.SemaphoreType.DMA((2,)),
             pltpu.SemaphoreType.DMA((7,)),
+            pltpu.SemaphoreType.DMA((4,)),
         ],
         compiler_params=pltpu.CompilerParams(collective_id=number, has_side_effects=True, vmem_limit_bytes=52 << 20),
         name="place%d" % capacity,
@@ -286,13 +313,12 @@
 
 
 def per_device(prior_gate_weight, left_factor, right_factor, refit_expert_index, placement):
-    table, needed = make_plan(refit_expert_index, placement)
+    table, branch = make_plan(refit_expert_index, placement)
     operands = (table, prior_gate_weight, jnp.swapaxes(left_factor, 1, 2), right_factor)
     if len(CAPACITIES) == 1:
         return place(CAPACITIES[0], 0, *operands)
-    branch = sum((needed[0] > capacity).astype(jnp.int32) for capacity in CAPACITIES[:-1])
     branches = [functools.partial(place, capacity, n) for n, capacity in enumerate(CAPACITIES)]
-    return lax.switch(branch, branches, *operands)
+    return lax.switch(branch[0], branches, *operands)
 
 
 def solution(mesh):

time: 158 us -> 144 us (0.911)
  Pallas kernels: 151 us -> 140 us
  between operations: 3.26 us -> 0.67 us
    pallas_call x1, Pallas kernels: 149 us -> 138 us  [place(): pl.pallas_call(functools.partial(place_kernel, capacity, steps), out_shap...]
where the time goes in v4:
time: 144 us
  Pallas kernels  140 us (97%)
  local copies, waits for them, and re-layouts  3.05 us (2%)
    pallas_call x1, Pallas kernels, place(): pl.pallas_call(functools.partial(place_kernel, capacity, steps), out_shap...  138 us
    unnamed x1, local copies, waits for them, and re-layouts  3.05 us

profile of v4, /device:TPU:1, one launch (start us, length us, event | category | flops | bytes accessed | tf_op | source)
XLA Modules:
  0.0 143.5 jit_solution(3931970312226764136)
XLA Ops:
  0.0 2.0 %plan.1 = (s32[128]{0:T(128)S(1)}, s32[1]{0:T(128)}) custom-call(s32[32]{0:T(128)} %refit.1, s32[64]{0:T(128)} %placement.1), custom_call_target="tpu_custom_call" | custom-call | tf_op jit(solution)/shard_map/plan/pallas_call | solution.py:82
  2.7 137.8 %conditional.1 = (bf16[2,7168,256]{2,1,0:T(8,128)(2,1)S(1)}) conditional(s32[]{:T(128)} %bitcast.6, (bf16[1,7168,256]{2,1,0:T(8,128)(2,1)}, s32[128]{0:T(128)S(1)}, bf16[1,64,7168]{2,1,0:T(8,128)(2,1)}, bf16[1,64,256]{2,1,0:T(8,128)(2,1)}) %tuple.36, (bf16[1,7168,256]{2,1,0:T(8,128)(2,1)}, s32[128]{0:T(128)S(1)}, ...), branch_computations={%region_0.0_spmd, %region_1.0_spmd, %region_2.0_spmd, %region_3.0_... | conditional | bytes 8 | solution.py:321
  2.7 137.8 %place11.1 = bf16[2,7168,256]{2,1,0:T(8,128)(2,1)S(1)} custom-call(s32[128]{0:T(128)S(1)} %get-tuple-element.64.table, bf16[4,1792,256]{2,1,0:T(8,128)(2,1)} %bitcast.9, bf16[1,64,7168]{2,1,0:T(8,128)(2,1)} %get-tuple-element.66.left_all, bf16[1,64,256]{2,1,0:T(8,128)(2,1)} %get-tuple-element.108.right_all), custom_call_target="tpu_custom_call" | custom-call | tf_op jit(solution)/shard_map/cond/branch_1_fun/place11/pallas_call | solution.py:282
  140.5 3.1 %copy.31 = bf16[2,7168,256]{2,1,0:T(8,128)(2,1)} copy(bf16[2,7168,256]{2,1,0:T(8,128)(2,1)S(1)} %get-tuple-element.88) | data formatting | bytes 14680064

commit v5 on v4

--- a/solution.py
+++ b/solution.py
@@ -17,10 +17,10 @@
 ZERO = 32
 RING = 8
 GROUP = 8
-EDGE_SEND = 3
-PICK_MID = 4
-FINISH_MIDDLE = 7
-FINISH_EDGE = 10
+EDGE_SEND = 2
+PICK_MID = 3
+FINISH_MIDDLE = 6
+FINISH_EDGE = 9
 LAST = FINISH_EDGE + 1
 SMEM = pltpu.SMEM
 VMEM = pltpu.VMEM
@@ -81,7 +81,7 @@
 def make_plan(refit, placement):
     return pl.pallas_call(
         plan_kernel,
-        out_shape=(jax.ShapeDtypeStruct((128,), jnp.int32), jax.ShapeDtypeStruct((1,), jnp.int32)),
+        out_shape=(SMEM((128,), jnp.int32), jax.ShapeDtypeStruct((1,), jnp.int32)),
         in_specs=[pl.BlockSpec(memory_space=SMEM)] * 2,
         out_specs=(pl.BlockSpec(memory_space=SMEM),) * 2,
         scratch_shapes=[SMEM((256,), jnp.int32), SMEM((64,), jnp.int32), SMEM((128,), jnp.int32), SMEM((40,), jnp.int32)],
@@ -125,11 +125,17 @@
                 own[front * part + n, g, c] = jnp.where(c == 0, first, second)
                 sib[front * part + n, g] = jnp.where(c == 0, second, first)
 
+    def exchange(part):
+        for n in range(front):
+            t = front * part + n
+            remote(sib.at[t], own.at[t, :, c], 0, sib_in.at[t], sibling).start()
+
+    def compute_ahead(i):
+        compute(i + 2)
+
         @pl.when(i % 2 == 1)
         def _():
-            for n in range(front):
-                t = front * part + n
-                remote(sib.at[t], own.at[t, :, c], 0, sib_in.at[t], sibling).start()
+            exchange((i + 2) // 2)
 
     def scatter(i):
         for n in range(front // 2):
@@ -223,7 +229,11 @@
         work[w, ZERO] = jnp.zeros((size, width), jnp.bfloat16)
     for fetch in fetches[:3]:
         fetch.wait()
+    compute(0)
+    compute(1)
     pl.semaphore_wait(barrier, lax.select(middle, 6, 5))
+    exchange(0)
+    fetches[3].wait()
 
     def stage(i, delay, count, body, role=None):
         t = i - delay
@@ -235,12 +245,8 @@
 
     @pl.loop(0, steps + LAST)
     def _(i):
-        @pl.when(i == 2)
-        def _():
-            fetches[3].wait()
-
-        stage(i, 0, 2 * steps // front, compute)
-        stage(i, 2, 2 * steps // front, scatter)
+        stage(i, 0, 2 * steps // front - 2, compute_ahead)
+        stage(i, 1, 2 * steps // front, scatter)
         stage(i, EDGE_SEND, steps, edge_send, edge)
         stage(i, PICK_MID, steps, pick_mid, middle)
         stage(i, FINISH_MIDDLE, steps, finish_middle, middle)

time: 144 us -> 153 us (1.062)
  Pallas kernels: 140 us -> 149 us
    pallas_call x1, Pallas kernels: 138 us -> 147 us  [place(): pl.pallas_call(functools.partial(place_kernel, capacity, steps), out_shap...]
where the time goes in v5:
time: 153 us; the launch traced here: 152 us
  Pallas kernels  149 us (97%)
  local copies, waits for them, and re-layouts  3.05 us (2%)
    pallas_call x1, Pallas kernels, place(): pl.pallas_call(functools.partial(place_kernel, capacity, steps), out_shap...  147 us

profile of v5, /device:TPU:1, one launch (start us, length us, event | category | flops | bytes accessed | tf_op | source)
XLA Modules:
  0.0 152.4 jit_solution(14988645661522282204)
XLA Ops:
  0.0 1.9 %plan.1 = (s32[128]{0:T(128)S(4)}, s32[1]{0:T(128)}) custom-call(s32[32]{0:T(128)} %refit.1, s32[64]{0:T(128)} %placement.1), custom_call_target="tpu_custom_call" | custom-call | tf_op jit(solution)/shard_map/plan/pallas_call | solution.py:82
  2.6 146.8 %conditional.1 = (bf16[2,7168,256]{2,1,0:T(8,128)(2,1)S(1)}) conditional(s32[]{:T(128)} %bitcast.6, (bf16[1,7168,256]{2,1,0:T(8,128)(2,1)}, s32[128]{0:T(128)S(4)}, bf16[1,64,7168]{2,1,0:T(8,128)(2,1)}, bf16[1,64,256]{2,1,0:T(8,128)(2,1)}) %tuple.36, (bf16[1,7168,256]{2,1,0:T(8,128)(2,1)}, s32[128]{0:T(128)S(4)}, ...), branch_computations={%region_0.0_spmd, %region_1.0_spmd, %region_2.0_spmd, %region_3.0_... | conditional | bytes 8 | solution.py:327
  2.6 146.7 %place12.1 = bf16[2,7168,256]{2,1,0:T(8,128)(2,1)S(1)} custom-call(s32[128]{0:T(128)S(4)} %get-tuple-element.68.table, bf16[4,1792,256]{2,1,0:T(8,128)(2,1)} %bitcast.10, bf16[1,64,7168]{2,1,0:T(8,128)(2,1)} %get-tuple-element.70.left_all, bf16[1,64,256]{2,1,0:T(8,128)(2,1)} %get-tuple-element.109.right_all), custom_call_target="tpu_custom_call" | custom-call | tf_op jit(solution)/shard_map/cond/branch_2_fun/place12/pallas_call | solution.py:288
  149.4 3.1 %copy.31 = bf16[2,7168,256]{2,1,0:T(8,128)(2,1)} copy(bf16[2,7168,256]{2,1,0:T(8,128)(2,1)S(1)} %get-tuple-element.88) | data formatting | bytes 14680064
